TPU v7x, 32 devices: a whole 2x2x4 slice. The times are simulated.
32 devices in a mesh: group: 8 (over z, core), inner: 4 (over y, x).
Axes of the slice: x: 2, y: 2, z: 4, core: 2. Of those that a mesh axis runs over, the one named last changes fastest.
Arguments:
- embeddings: bfloat16 [16384, 256], P(('group', 'inner')), may hold values from -6 to 6
- cluster_id: int32 [16384], P(('group', 'inner')), may hold values from 0 to 511, as said below
- order_rank: int32 [16384], P(('group', 'inner')), may hold values from 0 to 16383, each once
- send_slot: int32 [16384], P(('group', 'inner')), may hold values from 0 to 1023, as said below
- usable: int32 [16384], P(('group', 'inner')), may hold values 0 or 1
Outputs:
- best_cosine: float32 [16384], P(('group', 'inner'))
Inputs may be any that keep to these rules, and one draw needn't show every extreme that they name: send_slot // 128 is the group that owns a row and send_slot % 128 its slot among the 128 slots from its device to that group; no two rows of one device share a value. For each group and each index of inner, the rows sent to that group by the 8 devices with that inner index number at most 768, and some such count equals 768 in every draw; half of the devices fill all 128 slots to some group. A row owned by group g has a cluster id from g * 64 to (g + 1) * 64 - 1. Among the rows sent to one group by the devices of one inner index, at most 192 have any one value of cluster_id % 4, and that count is reached in every draw.
All inputs are finite; a program needn't handle non-finite values. No bound on the sum of `usable` on one device may be relied on, other than what follows from the above.
Results may differ from a plain program's by a relative error of at most 0.0016.
Values may be sent and summed in bfloat16 or wider, within the bound.
A program may use at most 64 MiB of HBM per device.

v0:
```python
import jax
import jax.numpy as jnp
from jax import lax
from jax.sharding import PartitionSpec as P


def unit_rows(embeddings):
    values = embeddings.astype(jnp.float32)
    inverse = lax.rsqrt(jnp.sum(values * values, axis=1, keepdims=True) + 1e-06)
    return (values * inverse).astype(jnp.bfloat16)


def fold_keys(running, pieces, queries, query_tags, shard_rows):
    key_rows, key_tags = pieces
    key_count = key_rows.shape[0]
    block_rows = min(key_count, shard_rows)
    blocks = key_count // block_rows
    row_blocks = key_rows.reshape(blocks, block_rows, key_rows.shape[1])
    tag_blocks = key_tags.reshape(blocks, block_rows, key_tags.shape[1])
    query_cluster = query_tags[:, 0][:, None]
    query_order = query_tags[:, 2][:, None]

    def absorb(current, pair_block):
        block_keys, block_tags = pair_block
        scores = lax.dot_general(
            queries, block_keys, (((1,), (1,)), ((), ())), preferred_element_type=jnp.float32
        )
        matched = (query_cluster == block_tags[:, 1][None, :]) & (
            block_tags[:, 2][None, :] < query_order
        )
        return (jnp.maximum(current, jnp.max(jnp.where(matched, scores, -1.0), axis=1)), None)

    result, _ = lax.scan(absorb, running, (row_blocks, tag_blocks))
    return result


def local(embeddings, cluster_id, order_rank, send_slot, usable):
    groups = lax.axis_size("group")
    row_count = embeddings.shape[0]
    capacity = 2 * row_count // groups
    slot_total = groups * capacity
    normed = unit_rows(embeddings)
    member_cluster = jnp.where(usable > 0, cluster_id, -1)
    tag_rows = jnp.stack([cluster_id, member_cluster, order_rank], axis=1)
    outgoing = jnp.zeros((slot_total, normed.shape[1]), jnp.bfloat16).at[send_slot].set(normed)
    out_tags = jnp.full((slot_total, 3), -1, jnp.int32).at[send_slot].set(tag_rows)
    arrived, arrived_tags = (
        lax.all_to_all(
            outgoing.reshape(groups, capacity, normed.shape[1]),
            "group",
            split_axis=0,
            concat_axis=0,
            tiled=True,
        ),
        lax.all_to_all(
            out_tags.reshape(groups, capacity, 3), "group", split_axis=0, concat_axis=0, tiled=True
        ),
    )
    arrived = arrived.reshape(slot_total, normed.shape[1])
    arrived_tags = arrived_tags.reshape(slot_total, 3)
    best_score = fold_keys(
        jnp.full((slot_total,), -1.0, jnp.float32),
        (
            lax.all_gather(arrived, "inner", axis=0, tiled=True),
            lax.all_gather(arrived_tags, "inner", axis=0, tiled=True),
        ),
        arrived,
        arrived_tags,
        slot_total,
    )
    returned = lax.all_to_all(
        best_score.reshape(groups, capacity), "group", split_axis=0, concat_axis=0, tiled=True
    )
    return returned.reshape(slot_total)[send_slot]


def solution(mesh):
    placed = (
        P(("group", "inner"), None),
        P(("group", "inner")),
        P(("group", "inner")),
        P(("group", "inner")),
        P(("group", "inner")),
    )
    return jax.shard_map(
        local, mesh=mesh, in_specs=placed, out_specs=P(("group", "inner")), check_vma=False
    )
```

profile of v0, /device:TPU:0, one launch (start us, length us, event | category | flops | bytes accessed | tf_op | source)
XLA Modules:
  0.0 101.0 jit_solution(7273263750019689542)
XLA Ops:
  6.5 0.0 copy-start.1
  6.5 0.0 copy-start
  6.5 0.0 copy-start.2
  6.5 0.0 all-gather.2.cloned.1.call-start
  6.5 0.7 compare_select_fusion
  7.3 1.1 %fusion.4 = f32[512]{0:T(512)S(1)} fusion(bf16[512,256]{1,0:T(8,128)(2,1)} %param.7), kind=kLoop, calls=%fused_computation.12 | loop fusion | flops 392704 | bytes 264192 | tf_op jit(solution)/shard_map/reduce_sum | solution.py:9
  8.4 3.0 %scatter_custom_fusion.1 = bf16[1024,256]{1,0:T(8,128)(2,1)S(1)} fusion(s32[512]{0:T(512)S(1)} %compare_select_fusion, bf16[512,256]{1,0:T(8,128)(2,1)} %param.7, f32[512]{0:T(512)S(1)} %add_rsqrt_fusion, bf16[]{:T(256)} %constant.19.clone.1), kind=kCustom, calls=%fused_computation.14 | custom fusion | flops 393216 | bytes 788482 | tf_op jit(solution)/shard_map/scatter | solution.py:45
  11.4 21.6 %all_to_all.19 = bf16[8,128,256]{2,1,0:T(8,128)(2,1)} all-to-all(bf16[8,128,256]{2,1,0:T(8,128)(2,1)S(1)} %bitcast.44), channel_id=1, replica_groups=mesh['group'=8,'inner'=4] {'group'}, dimensions={0} | all-to-all | bytes 1048576 | tf_op jit(solution)/shard_map/all_to_all | solution.py:48
  33.0 0.0 all-gather.2.cloned.1.call-update
  33.0 0.0 copy-done.1
  33.0 0.0 copy-done
  33.0 0.0 copy-done.2
  33.0 0.1 copy.9
  33.2 1.8 %scatter_custom_fusion = s32[1024,3]{1,0:T(8,128)S(1)} fusion(s32[512]{0:T(512)S(1)} %compare_select_fusion, s32[512,3]{1,0:T(8,128)S(1)} %copy.9, s32[]{:T(128)} %constant.9.clone.1), kind=kCustom, calls=%fused_computation.17 | custom fusion | bytes 12292 | tf_op jit(solution)/shard_map/scatter | solution.py:46
  35.0 0.8 copy.10
  35.8 3.3 %all-to-all-start = ((s32[8,128,3]{1,2,0:T(4,128)}), s32[8,128,3]{1,2,0:T(4,128)S(1)}, u32[]{:S(2)}, u32[]{:S(2)}) async-start(s32[8,128,3]{1,2,0:T(4,128)} %copy.10), calls=%async_computation | async-start | bytes 32768 | tf_op jit(solution)/shard_map/all_to_all | solution.py:55
  39.2 5.6 %all-to-all-done = s32[8,128,3]{1,2,0:T(4,128)S(1)} async-done(((s32[8,128,3]{1,2,0:T(4,128)}), s32[8,128,3]{1,2,0:T(4,128)S(1)}, u32[]{:S(2)}, u32[]{:S(2)}) %all-to-all-start) | async-done | bytes 12320 | tf_op jit(solution)/shard_map/all_to_all | solution.py:55
  44.8 8.2 %all_gather.6 = s32[4096,3]{0,1:T(4,128)S(1)} all-gather(s32[1024,3]{0,1:T(4,128)S(1)} %bitcast.47), channel_id=1, replica_groups=mesh['group'=8,'inner'=4] {'inner'}, dimensions={0}, use_global_device_ids=true | all-gather | bytes 61440 | tf_op jit(solution)/shard_map/all_gather | solution.py:65
  53.0 14.5 %all-gather.2.cloned.1.call-done = bf16[4096,256]{1,0:T(8,128)(2,1)} async-done(((bf16[1024,256]{1,0:T(8,128)(2,1)}), bf16[4096,256]{1,0:T(8,128)(2,1)}) %all-gather.2.cloned.1.call-update) | async-done | bytes 2097168 | tf_op jit(solution)/shard_map/all_gather | solution.py:64
  67.5 13.0 %while.11 = (s32[]{:T(128)}, f32[1024]{0:T(1024)}, s32[1024,1]{0,1:T(1,128)S(1)}, s32[4,1024,3]{1,2,0:T(4,128)S(1)}, s32[1024,1]{0,1:T(1,128)S(1)}, /*index=5*/b...) while((s32[]{:T(128)}, f32[1024]{0:T(1024)}, ...), condition=%wide.region_5.6_spmd.clone, body=%wide.region_3.5_spmd.clone.sunk | while | flops 542114816 | bytes 1122923 | solution.py:33
  67.5 2.1 %fusion.22 = f32[1024]{0:T(1024)S(1)} fusion(bf16[1024,256]{1,0:T(8,128)(2,1)} %get-tuple-element.156, s32[1024]{0:T(1024)S(1)} %bitcast.53, s32[1024]{0:T(1024)S(1)} %bitcast.54, s32[1024]{0:T(1024)S(1)} %bitcast.50, s32[1024]{0:T(1024)S(1)} %bitcast.49, bf16[4,1024,256]{2,1,0:T(8,128)(2,1)} %get-tuple-element.155, s32[]{:T(128)} %get-tuple-element.141), kind=kOutput, calls=%fused_computation.4.clone.1 | convolution fusion | flops 542112768 | bytes 1069568 | tf_op jit(solution)/shard_map/while/body/eval_jaxpr/dot_general | solution.py:25
  69.7 0.6 select_maximum_fusion.2
  70.3 2.1 %fusion.22 = f32[1024]{0:T(1024)S(1)} fusion(bf16[1024,256]{1,0:T(8,128)(2,1)} %get-tuple-element.156, s32[1024]{0:T(1024)S(1)} %bitcast.53, s32[1024]{0:T(1024)S(1)} %bitcast.54, s32[1024]{0:T(1024)S(1)} %bitcast.50, s32[1024]{0:T(1024)S(1)} %bitcast.49, bf16[4,1024,256]{2,1,0:T(8,128)(2,1)} %get-tuple-element.155, s32[]{:T(128)} %get-tuple-element.141), kind=kOutput, calls=%fused_computation.4.clone.1 | convolution fusion | flops 542112768 | bytes 1069568 | tf_op jit(solution)/shard_map/while/body/eval_jaxpr/dot_general | solution.py:25
  72.4 1.3 %select_maximum_fusion.2 = f32[1024]{0:T(1024)} fusion(f32[1024]{0:T(1024)S(1)} %fusion.22, f32[1024]{0:T(1024)} %get-tuple-element.142, pred[]{:T(512)S(6)} %compare.3), kind=kLoop, calls=%fused_computation.8.clone.1 | loop fusion | flops 2048 | bytes 12289 | tf_op jit(solution)/shard_map/while/body/eval_jaxpr/max | solution.py:31
  73.7 2.1 %fusion.22 = f32[1024]{0:T(1024)S(1)} fusion(bf16[1024,256]{1,0:T(8,128)(2,1)} %get-tuple-element.156, s32[1024]{0:T(1024)S(1)} %bitcast.53, s32[1024]{0:T(1024)S(1)} %bitcast.54, s32[1024]{0:T(1024)S(1)} %bitcast.50, s32[1024]{0:T(1024)S(1)} %bitcast.49, bf16[4,1024,256]{2,1,0:T(8,128)(2,1)} %get-tuple-element.155, s32[]{:T(128)} %get-tuple-element.141), kind=kOutput, calls=%fused_computation.4.clone.1 | convolution fusion | flops 542112768 | bytes 1069568 | tf_op jit(solution)/shard_map/while/body/eval_jaxpr/dot_general | solution.py:25
  75.8 1.3 %select_maximum_fusion.2 = f32[1024]{0:T(1024)} fusion(f32[1024]{0:T(1024)S(1)} %fusion.22, f32[1024]{0:T(1024)} %get-tuple-element.142, pred[]{:T(512)S(6)} %compare.3), kind=kLoop, calls=%fused_computation.8.clone.1 | loop fusion | flops 2048 | bytes 12289 | tf_op jit(solution)/shard_map/while/body/eval_jaxpr/max | solution.py:31
  77.1 2.1 %fusion.22 = f32[1024]{0:T(1024)S(1)} fusion(bf16[1024,256]{1,0:T(8,128)(2,1)} %get-tuple-element.156, s32[1024]{0:T(1024)S(1)} %bitcast.53, s32[1024]{0:T(1024)S(1)} %bitcast.54, s32[1024]{0:T(1024)S(1)} %bitcast.50, s32[1024]{0:T(1024)S(1)} %bitcast.49, bf16[4,1024,256]{2,1,0:T(8,128)(2,1)} %get-tuple-element.155, s32[]{:T(128)} %get-tuple-element.141), kind=kOutput, calls=%fused_computation.4.clone.1 | convolution fusion | flops 542112768 | bytes 1069568 | tf_op jit(solution)/shard_map/while/body/eval_jaxpr/dot_general | solution.py:25
  79.2 1.3 %select_maximum_fusion.2 = f32[1024]{0:T(1024)} fusion(f32[1024]{0:T(1024)S(1)} %fusion.22, f32[1024]{0:T(1024)} %get-tuple-element.142, pred[]{:T(512)S(6)} %compare.3), kind=kLoop, calls=%fused_computation.8.clone.1 | loop fusion | flops 2048 | bytes 12289 | tf_op jit(solution)/shard_map/while/body/eval_jaxpr/max | solution.py:31
  80.5 4.6 %all-to-all-start.2 = ((f32[8,1,128]{2,1,0:T(1,128)}), f32[8,1,128]{2,1,0:T(1,128)S(1)}, u32[]{:S(2)}, u32[]{:S(2)}) async-start(f32[8,1,128]{2,1,0:T(1,128)} %bitcast.9), calls=%async_computation.2 | async-start | bytes 8192 | tf_op jit(solution)/shard_map/all_to_all | solution.py:71
  85.1 5.6 %all-to-all-done.2 = f32[8,1,128]{2,1,0:T(1,128)S(1)} async-done(((f32[8,1,128]{2,1,0:T(1,128)}), f32[8,1,128]{2,1,0:T(1,128)S(1)}, u32[]{:S(2)}, u32[]{:S(2)}) %all-to-all-start.2) | async-done | bytes 4128 | tf_op jit(solution)/shard_map/all_to_all | solution.py:71
  90.7 3.4 %gather_fusion = f32[512]{0:T(512)} fusion(f32[1024]{0:T(1024)S(1)} %bitcast.41, s32[1024]{0:T(1024)S(1)} %pad_clamp_fusion), kind=kCustom, calls=%fused_computation | custom fusion | bytes 6144 | tf_op jit(solution)/shard_map/gather | solution.py:74
  (14 shorter events, 0.1 us)
Async XLA Ops:
  6.5 26.4 %copy-start.1 = (s32[512]{0:T(512)S(1)}, s32[512]{0:T(512)}, u32[]{:S(2)}) copy-start(s32[512]{0:T(512)} %param.11) | copy-start | bytes 6148
  6.5 26.5 %copy-start = (s32[512]{0:T(512)S(1)}, s32[512]{0:T(512)}, u32[]{:S(2)}) copy-start(s32[512]{0:T(512)} %param.8) | copy-start | bytes 6148
  6.5 26.5 %copy-start.2 = (s32[512]{0:T(512)S(1)}, s32[512]{0:T(512)}, u32[]{:S(2)}) copy-start(s32[512]{0:T(512)} %param.9) | copy-start | bytes 6148
  6.5 61.0 %all-gather.2.cloned.1.call-start = ((), (), s32[]{:S(2)}) async-start(), calls=%async_computation.3 | async-start | bytes 2621440 | tf_op jit(solution)/shard_map/all_gather | solution.py:64
  35.8 8.9 %all-to-all-start = ((s32[8,128,3]{1,2,0:T(4,128)}), s32[8,128,3]{1,2,0:T(4,128)S(1)}, u32[]{:S(2)}, u32[]{:S(2)}) async-start(s32[8,128,3]{1,2,0:T(4,128)} %copy.10), calls=%async_computation | async-start | bytes 32768 | tf_op jit(solution)/shard_map/all_to_all | solution.py:55
  80.5 10.2 %all-to-all-start.2 = ((f32[8,1,128]{2,1,0:T(1,128)}), f32[8,1,128]{2,1,0:T(1,128)S(1)}, u32[]{:S(2)}, u32[]{:S(2)}) async-start(f32[8,1,128]{2,1,0:T(1,128)} %bitcast.9), calls=%async_computation.2 | async-start | bytes 8192 | tf_op jit(solution)/shard_map/all_to_all | solution.py:71
Sparse Core Ops, SparseCore 0:
  33.1 34.3 all-gather.1
where the time goes:
time: 101 us
  blocking collectives  29.8 us (30%)
  waiting for transfers between devices  25.7 us (25%)
  between operations  13.5 us (13%)
  other arithmetic  9.3 us (9%)
  matrix products  8.4 us (8%)
  starting transfers between devices  7.94 us (8%)
  local copies, waits for them, and re-layouts  6.26 us (6%)
    all_to_all x1, blocking collectives, local(): lax.all_to_all(outgoing.reshape(groups, capacity, normed.shape[1]), 'grou...  21.6 us
    all_gather x1, waiting for transfers between devices, local(): lax.all_gather(arrived, 'inner', axis=0, tiled=True)  14.5 us
    dot_general x4, matrix products, absorb(): lax.dot_general(queries, block_keys, (((1,), (1,)), ((), ())), preferred_...  8.4 us
    all_gather x1, blocking collectives, local(): lax.all_gather(arrived_tags, 'inner', axis=0, tiled=True)  8.23 us
    all_to_all x1, waiting for transfers between devices, local(): lax.all_to_all(out_tags.reshape(groups, capacity, 3), 'group', split_axis...  5.57 us
    all_to_all x1, waiting for transfers between devices, local(): lax.all_to_all(best_score.reshape(groups, capacity), 'group', split_axis=...  5.55 us
    all_to_all x1, starting transfers between devices, local(): lax.all_to_all(best_score.reshape(groups, capacity), 'group', split_axis=...  4.61 us
    max x4, other arithmetic, absorb(): jnp.maximum(current, jnp.max(jnp.where(matched, scores, -1.0), axis=1))  4.47 us
  transfers between devices with their start and end apart: 3, of which 3 were waited for; matrix products, arithmetic and copies ran while one was open for 3% of the time, Pallas kernels for 0%

commit v1 on v0

v1 whole, which is shorter than its diff:
```python
import functools

import jax
import jax.numpy as jnp
from jax import lax
from jax.experimental import pallas as pl
from jax.experimental.pallas import tpu as pltpu
from jax.sharding import PartitionSpec as P

MESH = pl.DeviceIdType.MESH
BASE = 64
HALF = 128
TAGS = 16


def round_up(value, step):
    return (value + step - 1) // step * step


def partner(me, k):
    result, bit = me, 1
    while bit <= k:
        if k & bit:
            result = result + bit * (1 - 2 * lax.rem(lax.div(me, bit), 2))
        bit *= 2
    return result


def split_rows(value):
    high = value.astype(jnp.bfloat16).astype(jnp.float32)
    rest = value - high
    mid = rest.astype(jnp.bfloat16).astype(jnp.float32)
    low = rest - mid
    row = lax.broadcasted_iota(jnp.int32, (TAGS, value.shape[1]), 0)
    parts = jnp.where(row == 0, high, jnp.where(row == 1, mid, jnp.where(row == 2, low, 0.0)))
    return parts.astype(jnp.bfloat16)


def join_rows(parts):
    return (parts[0:1] + parts[1:2]) + parts[2:3]


def one_hot(position, rows):
    row = lax.broadcasted_iota(jnp.int32, (rows, position.shape[1]), 0)
    return jnp.where(row == position, 1.0, 0.0).astype(jnp.bfloat16)


def dot_nt(a, b):
    return lax.dot_general(a, b, (((1,), (1,)), ((), ())), preferred_element_type=jnp.float32)


def dot_nn(a, b):
    return jnp.dot(a, b, preferred_element_type=jnp.float32)


def kernel(
    groups, inner, capacity, lanes, bin_rows, bin_lanes,
    emb_ref, cid_ref, rank_ref, slot_ref, use_ref, out_ref,
    place, pick, limit,
    tag_out, tag_in, row_out, row_in, tag2_out, tag2_in, row2_out, row2_in,
    best_out, best_in, back_out, back_in,
    tag_s, tag_r, row_s, row_r, tag2_s, tag2_r, row2_s, row2_r, best_s, best_r, back_s, back_r,
):
    rows, width = emb_ref.shape
    halves = width // HALF
    total = inner * bin_rows
    my_group, my_inner = lax.axis_index("group"), lax.axis_index("inner")
    group_of = [partner(my_group, k) for k in range(groups)]
    inner_of = [partner(my_inner, k) for k in range(inner)]

    barrier = pltpu.get_barrier_semaphore()
    for k in range(1, groups):
        pl.semaphore_signal(barrier, inc=1, device_id={"group": group_of[k]}, device_id_type=MESH)
    for k in range(1, inner):
        pl.semaphore_signal(barrier, inc=1, device_id={"inner": inner_of[k]}, device_id_type=MESH)

    def remote(src, dst, send, recv, axis, peer):
        return pltpu.make_async_remote_copy(
            src_ref=src, dst_ref=dst, send_sem=send, recv_sem=recv,
            device_id={axis: peer}, device_id_type=MESH,
        )

    order = list(range(groups - 2, 0, -2))
    order = [k for pair in order for k in (pair, pair + 1)] + [1]
    inner_order = list(range(inner - 1, 0, -1))
    tag_copy = {k: remote(tag_out.at[k], tag_in.at[k], tag_s.at[k], tag_r.at[k], "group", group_of[k]) for k in order}
    row_copy = {
        (h, k): remote(row_out.at[h, k], row_in.at[h, k], row_s.at[h, k], row_r.at[h, k], "group", group_of[k])
        for h in range(halves) for k in order
    }
    tag2_copy = {k: remote(tag2_out.at[k], tag2_in.at[k], tag2_s.at[k], tag2_r.at[k], "inner", inner_of[k]) for k in inner_order}
    row2_copy = {
        (h, k): remote(row2_out.at[h, k], row2_in.at[h, k], row2_s.at[h, k], row2_r.at[h, k], "inner", inner_of[k])
        for h in range(halves) for k in inner_order
    }
    best_copy = {k: remote(best_out.at[k], best_in.at[k], best_s.at[k], best_r.at[k], "inner", inner_of[k]) for k in inner_order}
    back_copy = {k: remote(back_out.at[k], back_in.at[k], back_s.at[k], back_r.at[k], "group", group_of[k]) for k in order}

    cluster = cid_ref[...]
    rank = rank_ref[...]
    slot = slot_ref[...]
    row = lax.broadcasted_iota(jnp.int32, (TAGS, rows), 0)
    tags = jnp.where(row == 0, jnp.bitwise_and(cluster, BASE - 1), 0)
    tags = jnp.where(row == 1, 1, tags)
    tags = jnp.where(row == 2, use_ref[...], tags)
    tags = jnp.where(row == 3, jnp.bitwise_and(rank, BASE - 1), tags)
    tags = jnp.where(row == 4, jnp.bitwise_and(jnp.right_shift(rank, 6), BASE - 1), tags)
    tags = jnp.where(row == 5, jnp.right_shift(rank, 12), tags)
    tags = tags.astype(jnp.float32).astype(jnp.bfloat16)

    for k in order + [0]:
        wanted = slot - group_of[k] * capacity
        if capacity < lanes:
            wanted = jnp.where(wanted < capacity, wanted, -1)
        hot = one_hot(wanted, lanes)
        place[k] = hot
        block = dot_nt(tags, hot).astype(jnp.bfloat16)
        if k:
            tag_out[k] = block
        else:
            tag_in[0] = block

    pl.semaphore_wait(barrier, groups + inner - 2)
    for k in order:
        tag_copy[k].start()

    values = emb_ref[...].astype(jnp.float32)
    inverse = lax.rsqrt(jnp.sum(values * values, axis=1, keepdims=True) + 1e-06)
    unit = (values * inverse).astype(jnp.bfloat16)
    for k in order + [0]:
        block = dot_nn(place[k], unit).astype(jnp.bfloat16)
        for h in range(halves):
            part = block[:, h * HALF:(h + 1) * HALF]
            if k:
                row_out[h, k] = part
            else:
                row_in[h, 0] = part
        if k:
            row_copy[0, k].start()
    for h in range(1, halves):
        for k in order:
            row_copy[h, k].start()

    before = jnp.where(
        lax.broadcasted_iota(jnp.int32, (lanes, lanes), 0) < lax.broadcasted_iota(jnp.int32, (lanes, lanes), 1),
        1.0, 0.0,
    ).astype(jnp.bfloat16)
    bin_pad = round_up(inner, TAGS)
    seen = jnp.zeros((bin_pad, 1), jnp.float32)
    for k in order:
        tag_copy[k].wait_recv()
    for k in range(groups):
        arrived = tag_in[k].astype(jnp.float32)
        residue = jnp.bitwise_and(arrived[0:1].astype(jnp.int32), inner - 1)
        filled = arrived[1:2] > 0.5
        relative = jnp.full_like(residue, -1)
        for j in range(inner):
            relative = jnp.where(filled & (residue == inner_of[j]), j, relative)
        member = one_hot(relative, bin_pad)
        member_f = member.astype(jnp.float32)
        spot = dot_nn(member, before) + seen
        seen = seen + jnp.sum(member_f, axis=1, keepdims=True)
        spot = jnp.sum(member_f * spot, axis=0, keepdims=True).astype(jnp.int32)
        goal = jnp.where(filled, relative * bin_rows + spot, -1)
        pick[:, k * lanes:(k + 1) * lanes] = one_hot(goal, total)
    arrived_tags = jnp.concatenate([tag_in[k] for k in range(groups)], axis=1)
    for k in inner_order + [0]:
        block = dot_nt(arrived_tags, pick[k * bin_rows:(k + 1) * bin_rows, :]).astype(jnp.bfloat16)
        if bin_rows < bin_lanes:
            block = jnp.concatenate([block, jnp.zeros((TAGS, bin_lanes - bin_rows), jnp.bfloat16)], axis=1)
        if k:
            tag2_out[k] = block
            tag2_copy[k].start()
        else:
            tag2_in[0] = block

    def forward(h):
        for k in order:
            row_copy[h, k].wait_recv()
        arrived_rows = row_in[h].reshape(groups * lanes, HALF)
        for k in inner_order + [0]:
            block = dot_nn(pick[k * bin_rows:(k + 1) * bin_rows, :], arrived_rows).astype(jnp.bfloat16)
            if k:
                row2_out[h, k] = block
                row2_copy[h, k].start()
            else:
                row2_in[h, 0] = block

    for h in range(halves - 1):
        forward(h)

    for k in inner_order:
        tag2_copy[k].wait_recv()
    same = lax.broadcasted_iota(jnp.int32, (bin_lanes, bin_lanes), 0) == lax.broadcasted_iota(
        jnp.int32, (bin_lanes, bin_lanes), 1
    )
    eye = jnp.where(same, 1.0, 0.0).astype(jnp.bfloat16)
    key_cluster, key_rank = [], []
    for k in range(inner):
        columns = dot_nt(eye, tag2_in[k])[:bin_rows]
        key_cluster.append(jnp.where(columns[:, 1:2] * columns[:, 2:3] > 0.5, columns[:, 0:1], -1.0))
        key_rank.append(columns[:, 3:4] + BASE * columns[:, 4:5] + (BASE * BASE) * columns[:, 5:6])
    for q in range(inner):
        lines = tag2_in[q].astype(jnp.float32)[:, :bin_rows]
        query_cluster = lines[0:1]
        query_rank = lines[3:4] + BASE * lines[4:5] + (BASE * BASE) * lines[5:6]
        for k in range(inner):
            matched = (key_cluster[k] == query_cluster) & (key_rank[k] < query_rank)
            limit[q, k * bin_rows:(k + 1) * bin_rows, :] = jnp.where(matched, 1e30, -1.0)

    forward(halves - 1)

    for h in range(halves):
        for k in inner_order:
            row2_copy[h, k].wait_recv()
    keys = jnp.concatenate([row2_in[h].reshape(total, HALF) for h in range(halves)], axis=1)
    for q in inner_order + [0]:
        queries = jnp.concatenate([row2_in[h, q] for h in range(halves)], axis=1)
        scores = jnp.minimum(dot_nt(keys, queries), limit[q])
        best = jnp.maximum(jnp.max(scores, axis=0, keepdims=True), -1.0)
        if bin_rows < bin_lanes:
            best = jnp.concatenate([best, jnp.zeros((1, bin_lanes - bin_rows), jnp.float32)], axis=1)
        best = jnp.broadcast_to(best, (8, bin_lanes))
        if q:
            best_out[q] = best
            best_copy[q].start()
        else:
            best_in[0] = best

    for k in inner_order:
        best_copy[k].wait_recv()
    spread = jnp.zeros((TAGS, groups * lanes), jnp.float32)
    for k in range(inner):
        parts = split_rows(best_in[k, 0:1, :])[:, :bin_rows]
        spread = spread + dot_nn(parts, pick[k * bin_rows:(k + 1) * bin_rows, :])
    spread = join_rows(spread)
    for k in order + [0]:
        block = jnp.broadcast_to(spread[:, k * lanes:(k + 1) * lanes], (8, lanes))
        if k:
            back_out[k] = block
            back_copy[k].start()
        else:
            back_in[0] = block

    for k in order:
        back_copy[k].wait_recv()
    parts = jnp.concatenate([split_rows(back_in[k, 0:1, :]) for k in range(groups)], axis=1)
    result = dot_nn(parts, place[...].reshape(groups * lanes, rows))
    out_ref[...] = join_rows(result)

    for copies in (tag_copy, row_copy, tag2_copy, row2_copy, best_copy, back_copy):
        for copy in copies.values():
            copy.wait_send()


def local(embeddings, cluster_id, order_rank, send_slot, usable):
    groups, inner = lax.axis_size("group"), lax.axis_size("inner")
    rows, width = embeddings.shape
    capacity = 2 * rows // groups
    lanes = round_up(capacity, 128)
    bin_rows = 3 * rows // 2 // inner
    bin_lanes = round_up(bin_rows, 128)
    halves = width // HALF
    total = inner * bin_rows
    bf16, f32 = jnp.bfloat16, jnp.float32
    dma = pltpu.SemaphoreType.DMA
    sems = []
    for shape in ((groups,), (halves, groups), (inner,), (halves, inner), (inner,), (groups,)):
        sems += [dma(shape), dma(shape)]
    out = pl.pallas_call(
        functools.partial(kernel, groups, inner, capacity, lanes, bin_rows, bin_lanes),
        out_shape=jax.ShapeDtypeStruct((1, rows), f32),
        in_specs=[pl.BlockSpec(memory_space=pltpu.VMEM)] * 5,
        out_specs=pl.BlockSpec(memory_space=pltpu.VMEM),
        scratch_shapes=[
            pltpu.VMEM((groups, lanes, rows), bf16),
            pltpu.VMEM((total, groups * lanes), bf16),
            pltpu.VMEM((inner, total, bin_rows), f32),
            pltpu.VMEM((groups, TAGS, lanes), bf16),
            pltpu.VMEM((groups, TAGS, lanes), bf16),
            pltpu.VMEM((halves, groups, lanes, HALF), bf16),
            pltpu.VMEM((halves, groups, lanes, HALF), bf16),
            pltpu.VMEM((inner, TAGS, bin_lanes), bf16),
            pltpu.VMEM((inner, TAGS, bin_lanes), bf16),
            pltpu.VMEM((halves, inner, bin_rows, HALF), bf16),
            pltpu.VMEM((halves, inner, bin_rows, HALF), bf16),
            pltpu.VMEM((inner, 8, bin_lanes), f32),
            pltpu.VMEM((inner, 8, bin_lanes), f32),
            pltpu.VMEM((groups, 8, lanes), f32),
            pltpu.VMEM((groups, 8, lanes), f32),
        ] + sems,
        compiler_params=pltpu.CompilerParams(
            collective_id=0, has_side_effects=True, vmem_limit_bytes=40 * 1024 * 1024
        ),
        name="dedup",
    )(
        embeddings,
        cluster_id.reshape(1, rows),
        order_rank.reshape(1, rows),
        send_slot.reshape(1, rows),
        usable.reshape(1, rows),
    )
    return out.reshape(rows)


def solution(mesh):
    placed = (
        P(("group", "inner"), None),
        P(("group", "inner")),
        P(("group", "inner")),
        P(("group", "inner")),
        P(("group", "inner")),
    )
    return jax.shard_map(
        local, mesh=mesh, in_specs=placed, out_specs=P(("group", "inner")), check_vma=False
    )
```

time: 101 us -> 36.1 us (0.36)
  Pallas kernels: 0 us -> 32.9 us
  blocking collectives: 29.8 us -> 0 us
  waiting for transfers between devices: 25.7 us -> 0 us
  between operations: 13.5 us -> 0.01 us
  other arithmetic: 9.3 us -> 0 us
  matrix products: 8.4 us -> 0 us
  starting transfers between devices: 7.94 us -> 0 us
  local copies, waits for them, and re-layouts: 6.26 us -> 2.92 us
    pallas_call x0 -> x1, Pallas kernels: none -> 32.9 us  [local(): pl.pallas_call(functools.partial(kernel, groups, inner, capacity, lanes,...]
    all_to_all x1 -> x0, blocking collectives: 21.6 us -> none  [local(): lax.all_to_all(outgoing.reshape(groups, capacity, normed.shape[1]), 'grou...]
    all_gather x1 -> x0, waiting for transfers between devices: 14.5 us -> none  [local(): lax.all_gather(arrived, 'inner', axis=0, tiled=True)]
    all_to_all x2 -> x0, waiting for transfers between devices: 11.1 us -> none  [the longest x1 5.57 us: local(): lax.all_to_all(out_tags.reshape(groups, capacity, 3), 'group', split_axis...]
    dot_general x4 -> x0, matrix products: 8.4 us -> none  [absorb(): lax.dot_general(queries, block_keys, (((1,), (1,)), ((), ())), preferred_...]
    all_gather x1 -> x0, blocking collectives: 8.23 us -> none  [local(): lax.all_gather(arrived_tags, 'inner', axis=0, tiled=True)]
    all_to_all x2 -> x0, starting transfers between devices: 7.94 us -> none  [the longest x1 4.61 us: local(): lax.all_to_all(best_score.reshape(groups, capacity), 'group', split_axis=...]
    max x4 -> x0, other arithmetic: 4.47 us -> none  [absorb(): jnp.maximum(current, jnp.max(jnp.where(matched, scores, -1.0), axis=1))]
  transfers between devices with their start and end apart: 3 -> 0, of which waited for: 3 -> 0; matrix products, arithmetic and copies ran while one was open for 3% -> 0% of each run, Pallas kernels for 0% -> 0%
where the time goes in v1:
time: 36.1 us; the launch traced here: 35.9 us
  Pallas kernels  32.9 us (91%)
  local copies, waits for them, and re-layouts  2.92 us (8%)
    pallas_call x1, Pallas kernels, local(): pl.pallas_call(functools.partial(kernel, groups, inner, capacity, lanes,...  32.9 us
    unnamed x11, local copies, waits for them, and re-layouts  2.92 us

profile of v1, /device:TPU:0, one launch (start us, length us, event | category | flops | bytes accessed | tf_op | source)
XLA Modules:
  0.0 35.9 jit_solution(15407280363218324336)
XLA Ops:
  0.0 0.0 copy-start.3
  0.0 0.0 copy-start.2
  0.0 0.0 copy-start.1
  0.0 0.7 %copy-done.3 = s32[512]{0:T(512)S(1)} copy-done((s32[512]{0:T(512)S(1)}, s32[512]{0:T(512)}, u32[]{:S(2)}) %copy-start.3) | copy-done | bytes 2072
  0.7 0.0 copy-done.2
  0.7 0.0 copy-done.1
  0.7 0.0 copy-start
  0.7 0.9 %copy-done = bf16[512,256]{1,0:T(8,128)(2,1)S(1)} copy-done((bf16[512,256]{1,0:T(8,128)(2,1)S(1)}, bf16[512,256]{1,0:T(8,128)(2,1)}, u32[]{:S(2)}) %copy-start) | copy-done | bytes 262168
  1.7 0.0 copy-start.4
  1.7 0.7 %copy-done.4 = s32[512]{0:T(512)S(1)} copy-done((s32[512]{0:T(512)S(1)}, s32[512]{0:T(512)}, u32[]{:S(2)}) %copy-start.4) | copy-done | bytes 2072
  2.3 32.9 %dedup.1 = f32[1,512]{1,0:T(1,128)S(1)} custom-call(bf16[512,256]{1,0:T(8,128)(2,1)S(1)} %copy-done, s32[1,512]{1,0:T(1,128)S(1)} %bitcast.6, s32[1,512]{1,0:T(1,128)S(1)} %bitcast.7, s32[1,512]{1,0:T(1,128)S(1)} %bitcast.8, s32[1,512]{1,0:T(1,128)S(1)} %bitcast.9), custom_call_target="tpu_custom_call" | custom-call | tf_op jit(solution)/shard_map/dedup/pallas_call | solution.py:270
  35.3 0.6 %copy.7 = f32[512]{0:T(512)} copy(f32[512]{0:T(512)S(1)} %bitcast.5) | data formatting | bytes 4096
Async XLA Ops:
  0.0 0.7 %copy-start.3 = (s32[512]{0:T(512)S(1)}, s32[512]{0:T(512)}, u32[]{:S(2)}) copy-start(s32[512]{0:T(512)} %param.8) | copy-start | bytes 6148
  0.0 0.7 %copy-start.2 = (s32[512]{0:T(512)S(1)}, s32[512]{0:T(512)}, u32[]{:S(2)}) copy-start(s32[512]{0:T(512)} %param.7) | copy-start | bytes 6148
  0.0 0.7 %copy-start.1 = (s32[512]{0:T(512)S(1)}, s32[512]{0:T(512)}, u32[]{:S(2)}) copy-start(s32[512]{0:T(512)} %param.6) | copy-start | bytes 6148
  0.7 0.9 %copy-start = (bf16[512,256]{1,0:T(8,128)(2,1)S(1)}, bf16[512,256]{1,0:T(8,128)(2,1)}, u32[]{:S(2)}) copy-start(bf16[512,256]{1,0:T(8,128)(2,1)} %emb_ref.1) | copy-start | bytes 786436
  1.7 0.7 %copy-start.4 = (s32[512]{0:T(512)S(1)}, s32[512]{0:T(512)}, u32[]{:S(2)}) copy-start(s32[512]{0:T(512)} %param.9) | copy-start | bytes 6148

commit v2 on v1

--- a/solution.py
+++ b/solution.py
@@ -55,11 +55,12 @@
 
 def kernel(
     groups, inner, capacity, lanes, bin_rows, bin_lanes,
-    emb_ref, cid_ref, rank_ref, slot_ref, use_ref, out_ref,
+    emb_hbm, cid_hbm, rank_hbm, slot_hbm, use_hbm, out_ref,
+    emb_ref, cid_ref, rank_ref, slot_ref, use_ref, load,
     place, pick, limit,
     tag_out, tag_in, row_out, row_in, tag2_out, tag2_in, row2_out, row2_in,
-    best_out, best_in, back_out, back_in,
-    tag_s, tag_r, row_s, row_r, tag2_s, tag2_r, row2_s, row2_r, best_s, best_r, back_s, back_r,
+    back_place, back_out, back_in,
+    tag_s, tag_r, row_s, row_r, tag2_s, tag2_r, row2_s, row2_r, back_s, back_r,
 ):
     rows, width = emb_ref.shape
     halves = width // HALF
@@ -68,11 +69,24 @@
     group_of = [partner(my_group, k) for k in range(groups)]
     inner_of = [partner(my_inner, k) for k in range(inner)]
 
+    order = list(range(groups - 2, 0, -2))
+    order = [k for pair in order for k in (pair, pair + 1)] + [1]
+    inner_order = list(range(inner - 1, 0, -1))
     barrier = pltpu.get_barrier_semaphore()
-    for k in range(1, groups):
+    for k in order:
         pl.semaphore_signal(barrier, inc=1, device_id={"group": group_of[k]}, device_id_type=MESH)
-    for k in range(1, inner):
+    for k in inner_order:
         pl.semaphore_signal(barrier, inc=1, device_id={"inner": inner_of[k]}, device_id_type=MESH)
+
+    slot_load, emb_load, cid_load, rank_load, use_load = [
+        pltpu.make_async_copy(src, dst, load.at[n])
+        for n, (src, dst) in enumerate(
+            ((slot_hbm, slot_ref), (emb_hbm, emb_ref), (cid_hbm, cid_ref), (rank_hbm, rank_ref), (use_hbm, use_ref))
+        )
+    ]
+    for copy in (slot_load, emb_load, cid_load, rank_load, use_load):
+        copy.start()
+
 
     def remote(src, dst, send, recv, axis, peer):
         return pltpu.make_async_remote_copy(
@@ -80,9 +94,6 @@
             device_id={axis: peer}, device_id_type=MESH,
         )
 
-    order = list(range(groups - 2, 0, -2))
-    order = [k for pair in order for k in (pair, pair + 1)] + [1]
-    inner_order = list(range(inner - 1, 0, -1))
     tag_copy = {k: remote(tag_out.at[k], tag_in.at[k], tag_s.at[k], tag_r.at[k], "group", group_of[k]) for k in order}
     row_copy = {
         (h, k): remote(row_out.at[h, k], row_in.at[h, k], row_s.at[h, k], row_r.at[h, k], "group", group_of[k])
@@ -93,12 +104,32 @@
         (h, k): remote(row2_out.at[h, k], row2_in.at[h, k], row2_s.at[h, k], row2_r.at[h, k], "inner", inner_of[k])
         for h in range(halves) for k in inner_order
     }
-    best_copy = {k: remote(best_out.at[k], best_in.at[k], best_s.at[k], best_r.at[k], "inner", inner_of[k]) for k in inner_order}
-    back_copy = {k: remote(back_out.at[k], back_in.at[k], back_s.at[k], back_r.at[k], "group", group_of[k]) for k in order}
-
+    back_copy = {
+        (j, k): pltpu.make_async_remote_copy(
+            src_ref=back_out.at[j, k], dst_ref=back_in.at[j, k], send_sem=back_s.at[j, k], recv_sem=back_r.at[j, k],
+            device_id=(group_of[k], inner_of[j]), device_id_type=MESH,
+        )
+        for j in inner_order + [0] for k in order + [0] if j or k
+    }
+
+    slot_load.wait()
+    slot = slot_ref[...]
+    for k in order + [0]:
+        wanted = slot - group_of[k] * capacity
+        if capacity < lanes:
+            wanted = jnp.where(wanted < capacity, wanted, -1)
+        place[k] = one_hot(wanted, lanes)
+
+    emb_load.wait()
+    values = emb_ref[...].astype(jnp.float32)
+    inverse = lax.rsqrt(jnp.sum(values * values, axis=1, keepdims=True) + 1e-06)
+    unit = (values * inverse).astype(jnp.bfloat16)
+
+    cid_load.wait()
+    rank_load.wait()
+    use_load.wait()
     cluster = cid_ref[...]
     rank = rank_ref[...]
-    slot = slot_ref[...]
     row = lax.broadcasted_iota(jnp.int32, (TAGS, rows), 0)
     tags = jnp.where(row == 0, jnp.bitwise_and(cluster, BASE - 1), 0)
     tags = jnp.where(row == 1, 1, tags)
@@ -109,25 +140,6 @@
     tags = tags.astype(jnp.float32).astype(jnp.bfloat16)
 
     for k in order + [0]:
-        wanted = slot - group_of[k] * capacity
-        if capacity < lanes:
-            wanted = jnp.where(wanted < capacity, wanted, -1)
-        hot = one_hot(wanted, lanes)
-        place[k] = hot
-        block = dot_nt(tags, hot).astype(jnp.bfloat16)
-        if k:
-            tag_out[k] = block
-        else:
-            tag_in[0] = block
-
-    pl.semaphore_wait(barrier, groups + inner - 2)
-    for k in order:
-        tag_copy[k].start()
-
-    values = emb_ref[...].astype(jnp.float32)
-    inverse = lax.rsqrt(jnp.sum(values * values, axis=1, keepdims=True) + 1e-06)
-    unit = (values * inverse).astype(jnp.bfloat16)
-    for k in order + [0]:
         block = dot_nn(place[k], unit).astype(jnp.bfloat16)
         for h in range(halves):
             part = block[:, h * HALF:(h + 1) * HALF]
@@ -135,11 +147,17 @@
                 row_out[h, k] = part
             else:
                 row_in[h, 0] = part
+        block = dot_nt(tags, place[k]).astype(jnp.bfloat16)
         if k:
-            row_copy[0, k].start()
-    for h in range(1, halves):
-        for k in order:
-            row_copy[h, k].start()
+            tag_out[k] = block
+        else:
+            tag_in[0] = block
+
+    pl.semaphore_wait(barrier, groups + inner - 2)
+    for k in order:
+        tag_copy[k].start()
+    for k in order:
+        row_copy[0, k].start()
 
     before = jnp.where(
         lax.broadcasted_iota(jnp.int32, (lanes, lanes), 0) < lax.broadcasted_iota(jnp.int32, (lanes, lanes), 1),
@@ -163,7 +181,11 @@
         spot = jnp.sum(member_f * spot, axis=0, keepdims=True).astype(jnp.int32)
         goal = jnp.where(filled, relative * bin_rows + spot, -1)
         pick[:, k * lanes:(k + 1) * lanes] = one_hot(goal, total)
-    arrived_tags = jnp.concatenate([tag_in[k] for k in range(groups)], axis=1)
+    arrived_tags = jnp.concatenate([tag_in[k] for k in range(groups)], axis=1).astype(jnp.float32)
+    row = lax.broadcasted_iota(jnp.int32, (TAGS, lanes), 0)
+    lane = lax.broadcasted_iota(jnp.int32, (TAGS, lanes), 1)
+    spots = [jnp.where(row == 6, lane, jnp.where(row == 7, k, 0)).astype(jnp.float32) for k in range(groups)]
+    arrived_tags = (arrived_tags + jnp.concatenate(spots, axis=1)).astype(jnp.bfloat16)
     for k in inner_order + [0]:
         block = dot_nt(arrived_tags, pick[k * bin_rows:(k + 1) * bin_rows, :]).astype(jnp.bfloat16)
         if bin_rows < bin_lanes:
@@ -187,6 +209,10 @@
                 row2_in[h, 0] = block
 
     for h in range(halves - 1):
+        for k in order:
+            row_copy[h, k].wait_send()
+        for k in order:
+            row_copy[h + 1, k].start()
         forward(h)
 
     for k in inner_order:
@@ -199,6 +225,9 @@
     for k in range(inner):
         columns = dot_nt(eye, tag2_in[k])[:bin_rows]
         key_cluster.append(jnp.where(columns[:, 1:2] * columns[:, 2:3] > 0.5, columns[:, 0:1], -1.0))
+        origin = jnp.where(columns[:, 1:2] > 0.5, columns[:, 6:7] + lanes * columns[:, 7:8], -1.0)
+        lane = lax.broadcasted_iota(jnp.int32, (bin_rows, groups * lanes), 1).astype(jnp.float32)
+        back_place[k] = jnp.where(lane == origin, 1.0, 0.0).astype(jnp.bfloat16)
         key_rank.append(columns[:, 3:4] + BASE * columns[:, 4:5] + (BASE * BASE) * columns[:, 5:6])
     for q in range(inner):
         lines = tag2_in[q].astype(jnp.float32)[:, :bin_rows]
@@ -218,37 +247,29 @@
         queries = jnp.concatenate([row2_in[h, q] for h in range(halves)], axis=1)
         scores = jnp.minimum(dot_nt(keys, queries), limit[q])
         best = jnp.maximum(jnp.max(scores, axis=0, keepdims=True), -1.0)
-        if bin_rows < bin_lanes:
-            best = jnp.concatenate([best, jnp.zeros((1, bin_lanes - bin_rows), jnp.float32)], axis=1)
-        best = jnp.broadcast_to(best, (8, bin_lanes))
-        if q:
-            best_out[q] = best
-            best_copy[q].start()
-        else:
-            best_in[0] = best
-
-    for k in inner_order:
-        best_copy[k].wait_recv()
-    spread = jnp.zeros((TAGS, groups * lanes), jnp.float32)
-    for k in range(inner):
-        parts = split_rows(best_in[k, 0:1, :])[:, :bin_rows]
-        spread = spread + dot_nn(parts, pick[k * bin_rows:(k + 1) * bin_rows, :])
-    spread = join_rows(spread)
-    for k in order + [0]:
-        block = jnp.broadcast_to(spread[:, k * lanes:(k + 1) * lanes], (8, lanes))
-        if k:
-            back_out[k] = block
-            back_copy[k].start()
-        else:
-            back_in[0] = block
-
-    for k in order:
-        back_copy[k].wait_recv()
-    parts = jnp.concatenate([split_rows(back_in[k, 0:1, :]) for k in range(groups)], axis=1)
-    result = dot_nn(parts, place[...].reshape(groups * lanes, rows))
+        spread = join_rows(dot_nn(split_rows(best), back_place[q]))
+        for k in order + [0]:
+            block = spread[:, k * lanes:(k + 1) * lanes]
+            if q or k:
+                back_out[q, k] = block
+                back_copy[q, k].start()
+            else:
+                back_in[0, 0] = block
+
+    for copy in back_copy.values():
+        copy.wait_recv()
+    parts = []
+    for k in range(groups):
+        line = back_in[0, k]
+        for j in range(1, inner):
+            line = line + back_in[j, k]
+        parts.append(split_rows(line))
+    result = dot_nn(jnp.concatenate(parts, axis=1), place[...].reshape(groups * lanes, rows))
     out_ref[...] = join_rows(result)
 
-    for copies in (tag_copy, row_copy, tag2_copy, row2_copy, best_copy, back_copy):
+    for k in order:
+        row_copy[halves - 1, k].wait_send()
+    for copies in (tag_copy, tag2_copy, row2_copy, back_copy):
         for copy in copies.values():
             copy.wait_send()
 
@@ -265,14 +286,20 @@
     bf16, f32 = jnp.bfloat16, jnp.float32
     dma = pltpu.SemaphoreType.DMA
     sems = []
-    for shape in ((groups,), (halves, groups), (inner,), (halves, inner), (inner,), (groups,)):
+    for shape in ((groups,), (halves, groups), (inner,), (halves, inner), (inner, groups)):
         sems += [dma(shape), dma(shape)]
     out = pl.pallas_call(
         functools.partial(kernel, groups, inner, capacity, lanes, bin_rows, bin_lanes),
         out_shape=jax.ShapeDtypeStruct((1, rows), f32),
-        in_specs=[pl.BlockSpec(memory_space=pltpu.VMEM)] * 5,
+        in_specs=[pl.BlockSpec(memory_space=pltpu.HBM)] * 5,
         out_specs=pl.BlockSpec(memory_space=pltpu.VMEM),
         scratch_shapes=[
+            pltpu.VMEM((rows, width), bf16),
+            pltpu.VMEM((1, rows), jnp.int32),
+            pltpu.VMEM((1, rows), jnp.int32),
+            pltpu.VMEM((1, rows), jnp.int32),
+            pltpu.VMEM((1, rows), jnp.int32),
+            dma((5,)),
             pltpu.VMEM((groups, lanes, rows), bf16),
             pltpu.VMEM((total, groups * lanes), bf16),
             pltpu.VMEM((inner, total, bin_rows), f32),
@@ -284,10 +311,9 @@
             pltpu.VMEM((inner, TAGS, bin_lanes), bf16),
             pltpu.VMEM((halves, inner, bin_rows, HALF), bf16),
             pltpu.VMEM((halves, inner, bin_rows, HALF), bf16),
-            pltpu.VMEM((inner, 8, bin_lanes), f32),
-            pltpu.VMEM((inner, 8, bin_lanes), f32),
-            pltpu.VMEM((groups, 8, lanes), f32),
-            pltpu.VMEM((groups, 8, lanes), f32),
+            pltpu.VMEM((inner, bin_rows, groups * lanes), bf16),
+            pltpu.VMEM((inner, groups, 1, lanes), f32),
+            pltpu.VMEM((inner, groups, 1, lanes), f32),
         ] + sems,
         compiler_params=pltpu.CompilerParams(
             collective_id=0, has_side_effects=True, vmem_limit_bytes=40 * 1024 * 1024

time: 36.1 us -> 34.5 us (0.956)
  Pallas kernels: 32.9 us -> 31.4 us
    pallas_call x1, Pallas kernels: 32.9 us -> 31.4 us  [local(): pl.pallas_call(functools.partial(kernel, groups, inner, capacity, lanes,...]
where the time goes in v2:
time: 34.5 us; the launch traced here: 34.3 us
  Pallas kernels  31.4 us (91%)
  local copies, waits for them, and re-layouts  2.92 us (8%)
    pallas_call x1, Pallas kernels, local(): pl.pallas_call(functools.partial(kernel, groups, inner, capacity, lanes,...  31.4 us
    unnamed x11, local copies, waits for them, and re-layouts  2.92 us

profile of v2, /device:TPU:0, one launch (start us, length us, event | category | flops | bytes accessed | tf_op | source)
XLA Modules:
  0.0 34.3 jit_solution(5703109321584228225)
XLA Ops:
  0.0 0.0 copy-start.3
  0.0 0.0 copy-start.2
  0.0 0.0 copy-start.1
  0.0 0.7 %copy-done.3 = s32[512]{0:T(512)S(1)} copy-done((s32[512]{0:T(512)S(1)}, s32[512]{0:T(512)}, u32[]{:S(2)}) %copy-start.3) | copy-done | bytes 2072
  0.7 0.0 copy-done.2
  0.7 0.0 copy-done.1
  0.7 0.0 copy-start
  0.7 0.9 %copy-done = bf16[512,256]{1,0:T(8,128)(2,1)S(1)} copy-done((bf16[512,256]{1,0:T(8,128)(2,1)S(1)}, bf16[512,256]{1,0:T(8,128)(2,1)}, u32[]{:S(2)}) %copy-start) | copy-done | bytes 262168
  1.7 0.0 copy-start.4
  1.7 0.7 %copy-done.4 = s32[512]{0:T(512)S(1)} copy-done((s32[512]{0:T(512)S(1)}, s32[512]{0:T(512)}, u32[]{:S(2)}) %copy-start.4) | copy-done | bytes 2072
  2.3 31.4 %dedup.1 = f32[1,512]{1,0:T(1,128)S(1)} custom-call(bf16[512,256]{1,0:T(8,128)(2,1)S(1)} %copy-done, s32[1,512]{1,0:T(1,128)S(1)} %bitcast.6, s32[1,512]{1,0:T(1,128)S(1)} %bitcast.7, s32[1,512]{1,0:T(1,128)S(1)} %bitcast.8, s32[1,512]{1,0:T(1,128)S(1)} %bitcast.9), custom_call_target="tpu_custom_call" | custom-call | tf_op jit(solution)/shard_map/dedup/pallas_call | solution.py:291
  33.7 0.6 %copy.7 = f32[512]{0:T(512)} copy(f32[512]{0:T(512)S(1)} %bitcast.5) | data formatting | bytes 4096
Async XLA Ops:
  0.0 0.7 %copy-start.3 = (s32[512]{0:T(512)S(1)}, s32[512]{0:T(512)}, u32[]{:S(2)}) copy-start(s32[512]{0:T(512)} %param.8) | copy-start | bytes 6148
  0.0 0.7 %copy-start.2 = (s32[512]{0:T(512)S(1)}, s32[512]{0:T(512)}, u32[]{:S(2)}) copy-start(s32[512]{0:T(512)} %param.7) | copy-start | bytes 6148
  0.0 0.7 %copy-start.1 = (s32[512]{0:T(512)S(1)}, s32[512]{0:T(512)}, u32[]{:S(2)}) copy-start(s32[512]{0:T(512)} %param.6) | copy-start | bytes 6148
  0.7 0.9 %copy-start = (bf16[512,256]{1,0:T(8,128)(2,1)S(1)}, bf16[512,256]{1,0:T(8,128)(2,1)}, u32[]{:S(2)}) copy-start(bf16[512,256]{1,0:T(8,128)(2,1)} %emb_hbm.1) | copy-start | bytes 786436
  1.7 0.7 %copy-start.4 = (s32[512]{0:T(512)S(1)}, s32[512]{0:T(512)}, u32[]{:S(2)}) copy-start(s32[512]{0:T(512)} %param.9) | copy-start | bytes 6148

commit v3 on v2

--- a/solution.py
+++ b/solution.py
@@ -147,11 +147,13 @@
                 row_out[h, k] = part
             else:
                 row_in[h, 0] = part
-        block = dot_nt(tags, place[k]).astype(jnp.bfloat16)
-        if k:
-            tag_out[k] = block
-        else:
-            tag_in[0] = block
+        block = dot_nt(tags, place[k])
+        lines = (block[0:1] + block[1:2], block[2:3], block[3:4] + BASE * block[4:5] + (BASE * BASE) * block[5:6])
+        for n, line in enumerate(lines):
+            if k:
+                tag_out[k, n] = line
+            else:
+                tag_in[0, n] = line
 
     pl.semaphore_wait(barrier, groups + inner - 2)
     for k in order:
@@ -165,12 +167,14 @@
     ).astype(jnp.bfloat16)
     bin_pad = round_up(inner, TAGS)
     seen = jnp.zeros((bin_pad, 1), jnp.float32)
+    arrived_tags = []
     for k in order:
         tag_copy[k].wait_recv()
     for k in range(groups):
-        arrived = tag_in[k].astype(jnp.float32)
-        residue = jnp.bitwise_and(arrived[0:1].astype(jnp.int32), inner - 1)
-        filled = arrived[1:2] > 0.5
+        arrived = tag_in[k, 0].astype(jnp.int32)
+        filled = arrived > 0
+        member_of = jnp.where(filled, arrived - 1, 0)
+        residue = jnp.bitwise_and(member_of, inner - 1)
         relative = jnp.full_like(residue, -1)
         for j in range(inner):
             relative = jnp.where(filled & (residue == inner_of[j]), j, relative)
@@ -181,11 +185,19 @@
         spot = jnp.sum(member_f * spot, axis=0, keepdims=True).astype(jnp.int32)
         goal = jnp.where(filled, relative * bin_rows + spot, -1)
         pick[:, k * lanes:(k + 1) * lanes] = one_hot(goal, total)
-    arrived_tags = jnp.concatenate([tag_in[k] for k in range(groups)], axis=1).astype(jnp.float32)
-    row = lax.broadcasted_iota(jnp.int32, (TAGS, lanes), 0)
-    lane = lax.broadcasted_iota(jnp.int32, (TAGS, lanes), 1)
-    spots = [jnp.where(row == 6, lane, jnp.where(row == 7, k, 0)).astype(jnp.float32) for k in range(groups)]
-    arrived_tags = (arrived_tags + jnp.concatenate(spots, axis=1)).astype(jnp.bfloat16)
+        rank = tag_in[k, 2].astype(jnp.int32)
+        row = lax.broadcasted_iota(jnp.int32, (TAGS, lanes), 0)
+        lane = lax.broadcasted_iota(jnp.int32, (TAGS, lanes), 1)
+        lines = jnp.where(row == 0, member_of, 0)
+        lines = jnp.where((row == 1) & filled, 1, lines)
+        lines = jnp.where(row == 2, tag_in[k, 1].astype(jnp.int32), lines)
+        lines = jnp.where(row == 3, jnp.bitwise_and(rank, BASE - 1), lines)
+        lines = jnp.where(row == 4, jnp.bitwise_and(jnp.right_shift(rank, 6), BASE - 1), lines)
+        lines = jnp.where(row == 5, jnp.right_shift(rank, 12), lines)
+        lines = jnp.where(row == 6, lane, lines)
+        lines = jnp.where(row == 7, k, lines)
+        arrived_tags.append(lines.astype(jnp.float32).astype(jnp.bfloat16))
+    arrived_tags = jnp.concatenate(arrived_tags, axis=1)
     for k in inner_order + [0]:
         block = dot_nt(arrived_tags, pick[k * bin_rows:(k + 1) * bin_rows, :]).astype(jnp.bfloat16)
         if bin_rows < bin_lanes:
@@ -303,8 +315,8 @@
             pltpu.VMEM((groups, lanes, rows), bf16),
             pltpu.VMEM((total, groups * lanes), bf16),
             pltpu.VMEM((inner, total, bin_rows), f32),
-            pltpu.VMEM((groups, TAGS, lanes), bf16),
-            pltpu.VMEM((groups, TAGS, lanes), bf16),
+            pltpu.VMEM((groups, 3, 1, lanes), f32),
+            pltpu.VMEM((groups, 3, 1, lanes), f32),
             pltpu.VMEM((halves, groups, lanes, HALF), bf16),
             pltpu.VMEM((halves, groups, lanes, HALF), bf16),
             pltpu.VMEM((inner, TAGS, bin_lanes), bf16),

time: 34.5 us -> 34.2 us (level)
  Pallas kernels: 31.4 us -> 31 us
where the time goes in v3:
time: 34.2 us; the launch traced here: 34 us
  Pallas kernels  31 us (91%)
  local copies, waits for them, and re-layouts  2.92 us (9%)
    pallas_call x1, Pallas kernels, local(): pl.pallas_call(functools.partial(kernel, groups, inner, capacity, lanes,...  31 us
    unnamed x11, local copies, waits for them, and re-layouts  2.92 us

profile of v3, /device:TPU:0, one launch (start us, length us, event | category | flops | bytes accessed | tf_op | source)
XLA Modules:
  0.0 34.0 jit_solution(4654230099007421481)
XLA Ops:
  0.0 0.0 copy-start.3
  0.0 0.0 copy-start.2
  0.0 0.0 copy-start.1
  0.0 0.7 %copy-done.3 = s32[512]{0:T(512)S(1)} copy-done((s32[512]{0:T(512)S(1)}, s32[512]{0:T(512)}, u32[]{:S(2)}) %copy-start.3) | copy-done | bytes 2072
  0.7 0.0 copy-done.2
  0.7 0.0 copy-done.1
  0.7 0.0 copy-start
  0.7 0.9 %copy-done = bf16[512,256]{1,0:T(8,128)(2,1)S(1)} copy-done((bf16[512,256]{1,0:T(8,128)(2,1)S(1)}, bf16[512,256]{1,0:T(8,128)(2,1)}, u32[]{:S(2)}) %copy-start) | copy-done | bytes 262168
  1.7 0.0 copy-start.4
  1.7 0.7 %copy-done.4 = s32[512]{0:T(512)S(1)} copy-done((s32[512]{0:T(512)S(1)}, s32[512]{0:T(512)}, u32[]{:S(2)}) %copy-start.4) | copy-done | bytes 2072
  2.3 31.0 %dedup.1 = f32[1,512]{1,0:T(1,128)S(1)} custom-call(bf16[512,256]{1,0:T(8,128)(2,1)S(1)} %copy-done, s32[1,512]{1,0:T(1,128)S(1)} %bitcast.6, s32[1,512]{1,0:T(1,128)S(1)} %bitcast.7, s32[1,512]{1,0:T(1,128)S(1)} %bitcast.8, s32[1,512]{1,0:T(1,128)S(1)} %bitcast.9), custom_call_target="tpu_custom_call" | custom-call | tf_op jit(solution)/shard_map/dedup/pallas_call | solution.py:303
  33.4 0.6 %copy.7 = f32[512]{0:T(512)} copy(f32[512]{0:T(512)S(1)} %bitcast.5) | data formatting | bytes 4096
Async XLA Ops:
  0.0 0.7 %copy-start.3 = (s32[512]{0:T(512)S(1)}, s32[512]{0:T(512)}, u32[]{:S(2)}) copy-start(s32[512]{0:T(512)} %param.8) | copy-start | bytes 6148
  0.0 0.7 %copy-start.2 = (s32[512]{0:T(512)S(1)}, s32[512]{0:T(512)}, u32[]{:S(2)}) copy-start(s32[512]{0:T(512)} %param.7) | copy-start | bytes 6148
  0.0 0.7 %copy-start.1 = (s32[512]{0:T(512)S(1)}, s32[512]{0:T(512)}, u32[]{:S(2)}) copy-start(s32[512]{0:T(512)} %param.6) | copy-start | bytes 6148
  0.7 0.9 %copy-start = (bf16[512,256]{1,0:T(8,128)(2,1)S(1)}, bf16[512,256]{1,0:T(8,128)(2,1)}, u32[]{:S(2)}) copy-start(bf16[512,256]{1,0:T(8,128)(2,1)} %emb_hbm.1) | copy-start | bytes 786436
  1.7 0.7 %copy-start.4 = (s32[512]{0:T(512)S(1)}, s32[512]{0:T(512)}, u32[]{:S(2)}) copy-start(s32[512]{0:T(512)} %param.9) | copy-start | bytes 6148

commit v4 on v3

--- a/solution.py
+++ b/solution.py
@@ -255,11 +255,14 @@
         for k in inner_order:
             row2_copy[h, k].wait_recv()
     keys = jnp.concatenate([row2_in[h].reshape(total, HALF) for h in range(halves)], axis=1)
+    bests = {}
     for q in inner_order + [0]:
         queries = jnp.concatenate([row2_in[h, q] for h in range(halves)], axis=1)
         scores = jnp.minimum(dot_nt(keys, queries), limit[q])
         best = jnp.maximum(jnp.max(scores, axis=0, keepdims=True), -1.0)
-        spread = join_rows(dot_nn(split_rows(best), back_place[q]))
+        bests[q] = best
+    for q in inner_order + [0]:
+        spread = join_rows(dot_nn(split_rows(bests[q]), back_place[q]))
         for k in order + [0]:
             block = spread[:, k * lanes:(k + 1) * lanes]
             if q or k:

time: 34.2 us -> 33.3 us (0.974)
  Pallas kernels: 31 us -> 30.2 us
    pallas_call x1, Pallas kernels: 31 us -> 30.2 us  [local(): pl.pallas_call(functools.partial(kernel, groups, inner, capacity, lanes,...]
where the time goes in v4:
time: 33.3 us; the launch traced here: 33.1 us
  Pallas kernels  30.2 us (91%)
  local copies, waits for them, and re-layouts  2.92 us (9%)
    pallas_call x1, Pallas kernels, local(): pl.pallas_call(functools.partial(kernel, groups, inner, capacity, lanes,...  30.2 us
    unnamed x11, local copies, waits for them, and re-layouts  2.92 us

profile of v4, /device:TPU:0, one launch (start us, length us, event | category | flops | bytes accessed | tf_op | source)
XLA Modules:
  0.0 33.1 jit_solution(15103565400919107303)
XLA Ops:
  0.0 0.0 copy-start.3
  0.0 0.0 copy-start.2
  0.0 0.0 copy-start.1
  0.0 0.7 %copy-done.3 = s32[512]{0:T(512)S(1)} copy-done((s32[512]{0:T(512)S(1)}, s32[512]{0:T(512)}, u32[]{:S(2)}) %copy-start.3) | copy-done | bytes 2072
  0.7 0.0 copy-done.2
  0.7 0.0 copy-done.1
  0.7 0.0 copy-start
  0.7 0.9 %copy-done = bf16[512,256]{1,0:T(8,128)(2,1)S(1)} copy-done((bf16[512,256]{1,0:T(8,128)(2,1)S(1)}, bf16[512,256]{1,0:T(8,128)(2,1)}, u32[]{:S(2)}) %copy-start) | copy-done | bytes 262168
  1.7 0.0 copy-start.4
  1.7 0.7 %copy-done.4 = s32[512]{0:T(512)S(1)} copy-done((s32[512]{0:T(512)S(1)}, s32[512]{0:T(512)}, u32[]{:S(2)}) %copy-start.4) | copy-done | bytes 2072
  2.3 30.2 %dedup.1 = f32[1,512]{1,0:T(1,128)S(1)} custom-call(bf16[512,256]{1,0:T(8,128)(2,1)S(1)} %copy-done, s32[1,512]{1,0:T(1,128)S(1)} %bitcast.6, s32[1,512]{1,0:T(1,128)S(1)} %bitcast.7, s32[1,512]{1,0:T(1,128)S(1)} %bitcast.8, s32[1,512]{1,0:T(1,128)S(1)} %bitcast.9), custom_call_target="tpu_custom_call" | custom-call | tf_op jit(solution)/shard_map/dedup/pallas_call | solution.py:306
  32.5 0.6 %copy.7 = f32[512]{0:T(512)} copy(f32[512]{0:T(512)S(1)} %bitcast.5) | data formatting | bytes 4096
Async XLA Ops:
  0.0 0.7 %copy-start.3 = (s32[512]{0:T(512)S(1)}, s32[512]{0:T(512)}, u32[]{:S(2)}) copy-start(s32[512]{0:T(512)} %param.8) | copy-start | bytes 6148
  0.0 0.7 %copy-start.2 = (s32[512]{0:T(512)S(1)}, s32[512]{0:T(512)}, u32[]{:S(2)}) copy-start(s32[512]{0:T(512)} %param.7) | copy-start | bytes 6148
  0.0 0.7 %copy-start.1 = (s32[512]{0:T(512)S(1)}, s32[512]{0:T(512)}, u32[]{:S(2)}) copy-start(s32[512]{0:T(512)} %param.6) | copy-start | bytes 6148
  0.7 0.9 %copy-start = (bf16[512,256]{1,0:T(8,128)(2,1)S(1)}, bf16[512,256]{1,0:T(8,128)(2,1)}, u32[]{:S(2)}) copy-start(bf16[512,256]{1,0:T(8,128)(2,1)} %emb_hbm.1) | copy-start | bytes 786436
  1.7 0.7 %copy-start.4 = (s32[512]{0:T(512)S(1)}, s32[512]{0:T(512)}, u32[]{:S(2)}) copy-start(s32[512]{0:T(512)} %param.9) | copy-start | bytes 6148
